TPU v7x, 32 devices: a whole 2x2x4 slice. The times are simulated.
32 devices in a mesh: region: 4 (over z), col: 8 (over y, x, core).
Axes of the slice: x: 2, y: 2, z: 4, core: 2. Of those that a mesh axis runs over, the one named last changes fastest.
Arguments:
- forcing: float32 [3, 256, 1024], P(None, 'region', 'col'), may hold values from 0.05 to 3
- river_storage: float32 [256, 1024], P('region', 'col'), may hold values from 0.1 to 4
- river_rate: float32 [256, 1024], P('region', 'col'), may hold values from 0.2 to 0.9
- flow_code: int32 [256, 1024], P('region', 'col'), may hold values from 1 to 128
- home_slot: int32 [32, 1024], P(('region', 'col')), may hold values from -1 to 1023, as said below
- home_offset: int32 [32, 1024], P(('region', 'col')), may hold values from 0 to 8184, as said below
- worker_list: int32 [15360], P(('region', 'col')), may hold values from 0 to 1023, as said below
- patch_cell: int32 [15360, 128], P(('region', 'col')), may hold values from 0 to 63, as said below
- patch_area: float32 [15360, 128], P(('region', 'col')), may hold values from 0.02 to 0.3
- canopy_water: float32 [15360, 128], P(('region', 'col')), may hold values from 0 to 1
- canopy_cap: float32 [15360, 128], P(('region', 'col')), may hold values from 0.1 to 2
- soil_water: float32 [15, 15360, 128], P(None, ('region', 'col')), may hold values from 0.05 to 0.5
- porosity: float32 [15, 15360, 128], P(None, ('region', 'col')), may hold values from 0.3 to 0.55
- drainage: float32 [15, 15360, 128], P(None, ('region', 'col')), may hold values from 0.02 to 0.8
Outputs:
- soil_new: float32 [15, 15360, 128], P(None, ('region', 'col'))
- canopy_new: float32 [15360, 128], P(('region', 'col'))
- cell_runoff: float32 [256, 1024], P('region', 'col')
- cell_evap: float32 [256, 1024], P('region', 'col')
- river_new: float32 [256, 1024], P('region', 'col')
Inputs may be any that keep to these rules, and one draw needn't show every extreme that they name: `home_slot`: A home's live block slots come first and hold w * 32 + k (worker w, position k), distinct within the home; -1 marks unused slots. A home has 1024, 512, 256 or 128 live blocks, each for a quarter of the homes; at most 32 of one home's blocks go to one worker, and the busiest homes send exactly 32 to every worker. `worker_list`: every slot of every worker holds a live block; h * 32 + k at block b of worker w means home_slot[h, j] = w * 32 + k for exactly one j. `home_offset`: the first home cell of a live block, row-major over the home's cells; 0 for unused slots. Offset plus patch_cell stays below 8192. `patch_cell`: never falling along a block.
All inputs are finite; a program needn't handle non-finite values.
Results may differ from a plain program's by a relative error of at most 0.000073.
Values sent between devices are 32-bit elements; how exact they have to be, the bound alone decides.
No kernel may reach another device: no remote copies, remote signals or barrier semaphores. Data moves between devices by JAX's collectives and lax.ppermute only.
A program may use at most 64 MiB of HBM per device.

v0:
```python
import functools

import jax
import jax.numpy as jnp
from jax import lax
from jax.experimental import pallas as pl
from jax.experimental.pallas import tpu as pltpu
from jax.sharding import PartitionSpec as P

ITERS = 4
WINDOW = 64
LANES = 128
MIB = 1024 * 1024
VMEM_LIMIT = 24 * MIB

directions = ((0, 1), (1, 1), (1, 0), (1, -1), (0, -1), (-1, -1), (-1, 0), (-1, 1))
axes = ("region", "col")


def iota(shape, dim):
    return lax.broadcasted_iota(jnp.int32, shape, dim)


def onehot(mask):
    return jnp.where(mask, jnp.float32(1.0), jnp.float32(0.0)).astype(jnp.bfloat16)


def lane_pick(values, index):
    return jnp.take_along_axis(values, index, axis=1, mode="promise_in_bounds")


def in_hbm(value):
    return pltpu.with_memory_space_constraint(value, pltpu.HBM)


def thirds(value):
    high = value.astype(jnp.bfloat16)
    rest = value - high.astype(jnp.float32)
    middle = rest.astype(jnp.bfloat16)
    low = (rest - middle.astype(jnp.float32)).astype(jnp.bfloat16)
    return high, middle, low


def halves(value):
    high = value.astype(jnp.bfloat16)
    return high, (value - high.astype(jnp.float32)).astype(jnp.bfloat16)


def matmul(a, b, a_dim=1, b_dim=0):
    return lax.dot_general(
        a, b, (((a_dim,), (b_dim,)), ((), ())), preferred_element_type=jnp.float32
    )


def slot_factors(slot, offset, homes, capacity):
    slots = slot.shape[1]
    worker = slot // capacity if capacity & (capacity - 1) else slot >> (capacity.bit_length() - 1)
    position = slot - worker * capacity
    by_worker = onehot(iota((homes, slots), 0) == worker)
    at_position = iota((capacity, slots), 0) == position
    row = jnp.where(at_position, ((offset >> 7) + 1).astype(jnp.float32), 0.0)
    lane = jnp.where(at_position, (offset & 127).astype(jnp.float32), 0.0)
    return by_worker, row.astype(jnp.bfloat16), lane.astype(jnp.bfloat16)


def slot_columns(slot, offset, homes, capacity, split=False):
    slots = slot.shape[1]
    by_worker, row, lane = slot_factors(slot, offset, homes, capacity)
    table = matmul(by_worker, jnp.concatenate([row, lane], axis=0), 1, 1)
    groups = 2 if split else 1
    spread = jnp.broadcast_to(
        table[:, None, :], (homes, capacity // groups, 2 * capacity)
    ).reshape(slots // groups, 2 * capacity)
    spread = jnp.concatenate([spread] * groups, axis=0)
    number = iota(spread.shape, 0)
    position = number % (capacity // groups) * groups + number // (slots // groups)
    place = position == iota(spread.shape, 1) % capacity
    kept = jnp.where(place, spread, 0.0).astype(jnp.bfloat16)
    shape = (2 * capacity, 2 * LANES)
    gather = onehot((iota(shape, 0) >= capacity) == (iota(shape, 1) >= LANES))
    columns = matmul(kept, gather).astype(jnp.int32)
    return columns[:, :LANES] - 1, columns[:, LANES:]


def slot_rows(slot, offset, homes, capacity):
    slots = slot.shape[1]
    by_worker, row, lane = slot_factors(slot, offset, homes, capacity)
    table = matmul(jnp.concatenate([row, lane], axis=0), by_worker, 1, 1).astype(jnp.bfloat16)
    number = iota((1, slots), 1)
    worker = number // capacity
    position = number - worker * capacity
    spread = matmul(table, onehot(iota((homes, slots), 0) == worker))
    at_position = iota((capacity, slots), 0) == position
    rows = jnp.sum(jnp.where(at_position, spread[:capacity], 0.0), axis=0, keepdims=True)
    lanes = jnp.sum(jnp.where(at_position, spread[capacity:], 0.0), axis=0, keepdims=True)
    return rows.astype(jnp.int32) - 1, lanes.astype(jnp.int32)


def pack_kernel(
    homes, capacity, slot_in, offset_in, forcing_in, out, slot, offset, forcing, row_of, lane_of,
    rain, ready,
):
    copies = [
        pltpu.make_async_copy(source, target, ready.at[i])
        for i, (source, target) in enumerate(
            ((slot_in, slot), (offset_in, offset), (forcing_in, forcing))
        )
    ]
    for copy in copies:
        copy.start()
    slots = slot.shape[1]
    pairs = capacity // 2
    lane_rows = forcing.shape[1]
    copies[0].wait()
    copies[1].wait()
    row_of[...], lane_of[...] = slot_columns(slot[...], offset[...], homes, capacity, True)
    copies[2].wait()
    parts = []
    for var in range(3):
        here = forcing[var]
        following = jnp.concatenate([here[1:], here[:1]], axis=0)
        parts += [here, following]
    table = jnp.concatenate(thirds(jnp.concatenate(parts, axis=1)), axis=0)
    chunk = 128
    here = iota((chunk, LANES), 1)
    for start in range(0, slots, chunk):
        odd = start >= slots // 2
        row = row_of[pl.ds(start, chunk), :]
        lane = lane_of[pl.ds(start, chunk), :]
        shape = (chunk, 3 * lane_rows)
        wide = jnp.concatenate([row, row], axis=1)[:, : 3 * lane_rows]
        pick = onehot(wide == iota(shape, 1) % lane_rows)
        rows = matmul(pick, table)
        after = here >= lane
        joined = [
            jnp.where(
                after,
                rows[:, 2 * var * LANES : (2 * var + 1) * LANES],
                rows[:, (2 * var + 1) * LANES : (2 * var + 2) * LANES],
            )
            for var in range(3)
        ]
        first = (here + lane) & 127
        second = (first + WINDOW) & 127
        losses = jnp.where(
            here < WINDOW, lane_pick(joined[1], first), lane_pick(joined[2], second)
        )
        base = start - slots // 2 if odd else start
        if odd:
            rains = jnp.where(
                here < WINDOW, rain[pl.ds(base, chunk), :], lane_pick(joined[0], second)
            )
        else:
            rain[pl.ds(base, chunk), :] = lane_pick(joined[0], first)
        for part in range(0, chunk, pairs):
            place = (base + part) * 3
            if odd:
                out[pl.ds(place + pairs, pairs), :] = rains[part : part + pairs]
                out[pl.ds(place + 2 * pairs, pairs), :] = losses[part : part + pairs]
            else:
                out[pl.ds(place, pairs), :] = losses[part : part + pairs]


def pack(homes, capacity, slot, offset, forcing):
    slots = slot.shape[1]
    return pl.pallas_call(
        functools.partial(pack_kernel, homes, capacity),
        in_specs=[pl.BlockSpec(memory_space=pltpu.HBM)] * 3,
        out_shape=jax.ShapeDtypeStruct((slots + slots // 2, LANES), jnp.float32),
        scratch_shapes=[
            pltpu.VMEM(slot.shape, jnp.int32),
            pltpu.VMEM(offset.shape, jnp.int32),
            pltpu.VMEM(forcing.shape, jnp.float32),
            pltpu.VMEM((slots, LANES), jnp.int32),
            pltpu.VMEM((slots, LANES), jnp.int32),
            pltpu.VMEM((slots // 2, LANES), jnp.float32),
            pltpu.SemaphoreType.DMA((3,)),
        ],
        compiler_params=pltpu.CompilerParams(vmem_limit_bytes=VMEM_LIMIT),
        cost_estimate=pl.CostEstimate(flops=10**9, bytes_accessed=2 * MIB, transcendentals=0),
        name="pack_forcing",
    )(in_hbm(slot), in_hbm(offset), in_hbm(forcing))


def unpack_plan_kernel(homes, capacity, lane_rows, slot, offset, code, place):
    slots = slot.shape[1]
    row, lane = slot_columns(slot[...], offset[...], homes, capacity)
    here = iota((slots, LANES), 1)
    index = (here - lane) & 127
    inside = (index < WINDOW) & (row >= 0)
    code[...] = jnp.where(inside, index + jnp.where(here >= lane, 0, LANES), -1)
    row_lane, _ = slot_rows(slot[...], offset[...], homes, capacity)
    place[...] = onehot(iota((lane_rows, slots), 0) == row_lane)


def unpack_plan(homes, capacity, lane_rows, slot, offset):
    slots = slot.shape[1]
    return pl.pallas_call(
        functools.partial(unpack_plan_kernel, homes, capacity, lane_rows),
        out_shape=(
            jax.ShapeDtypeStruct((slots, LANES), jnp.int32),
            jax.ShapeDtypeStruct((lane_rows, slots), jnp.bfloat16),
        ),
        compiler_params=pltpu.CompilerParams(vmem_limit_bytes=VMEM_LIMIT),
        cost_estimate=pl.CostEstimate(flops=10**9, bytes_accessed=2 * MIB, transcendentals=0),
        name="unpack_plan",
    )(slot, offset)


def strips_for_neighbours(state, rows):
    device = iota((rows, LANES), 0) // ITERS
    down = device // lax.axis_size("col") - lax.axis_index("region")
    right = device % lax.axis_size("col") - lax.axis_index("col")
    height, width = state.shape
    columns = jnp.transpose(state)
    empty = jnp.zeros((ITERS, LANES - height), jnp.float32)

    def repeated(strip):
        if strip.shape[1] < LANES:
            strip = jnp.concatenate([strip, empty], axis=1)
        return jnp.concatenate([strip] * (rows // ITERS), axis=0)

    near = (jnp.abs(down) <= 1).astype(jnp.int32)
    strips = jnp.zeros((rows, LANES), jnp.float32)
    strips = jnp.where((right == 0) & (down == 1), repeated(state[height - ITERS :]), strips)
    strips = jnp.where((right == 0) & (down == -1), repeated(state[:ITERS]), strips)
    strips = jnp.where((right == 1) & (near == 1), repeated(columns[width - ITERS :]), strips)
    return jnp.where((right == -1) & (near == 1), repeated(columns[:ITERS]), strips)


def cell_totals(arrived, code, place, first):
    lane_rows = place.shape[0]
    marks = code[...]
    window = lane_pick(arrived[...], (marks + first) & 127)
    placed = jnp.concatenate(
        [
            jnp.where((marks >= 0) & (marks < LANES), window, 0.0),
            jnp.where(marks >= LANES, window, 0.0),
        ],
        axis=1,
    )
    totals = matmul(place[...], jnp.concatenate(halves(placed), axis=1))
    totals = totals[:, :256] + totals[:, 256:]
    over = totals[:, LANES:]
    over = jnp.concatenate([over[lane_rows - 1 :], over[: lane_rows - 1]], axis=0)
    over = jnp.where(iota(over.shape, 0) == 0, 0.0, over)
    return totals[:, :LANES] + over


def unpack_runoff_kernel(arrived, code, place, river, _, runoff, storage, strips):
    total = cell_totals(arrived, code, place, 0)
    state = river[...] + total
    runoff[...] = total
    storage[...] = state
    strips[...] = strips_for_neighbours(state, strips.shape[0])


def unpack_runoff(homes, arrived, code, place, river, after):
    shape = jax.ShapeDtypeStruct((place.shape[0], LANES), jnp.float32)
    strips = jax.ShapeDtypeStruct((homes * ITERS, LANES), jnp.float32)
    return pl.pallas_call(
        unpack_runoff_kernel,
        in_specs=[pl.BlockSpec(memory_space=pltpu.VMEM)] * 4 + [pl.BlockSpec(memory_space=pl.ANY)],
        out_shape=(shape, shape, strips),
        compiler_params=pltpu.CompilerParams(vmem_limit_bytes=VMEM_LIMIT),
        cost_estimate=pl.CostEstimate(flops=10**9, bytes_accessed=1 * MIB, transcendentals=0),
        name="unpack_runoff",
    )(arrived, code, place, river, after)


def unpack_evap_kernel(arrived, code, place, evap):
    evap[...] = cell_totals(arrived, code, place, WINDOW)


def unpack_evap(arrived, code, place):
    return pl.pallas_call(
        unpack_evap_kernel,
        out_shape=jax.ShapeDtypeStruct((place.shape[0], LANES), jnp.float32),
        compiler_params=pltpu.CompilerParams(vmem_limit_bytes=VMEM_LIMIT),
        cost_estimate=pl.CostEstimate(flops=10**9, bytes_accessed=1 * MIB, transcendentals=0),
        name="unpack_evap",
    )(arrived, code, place)


def segment_plan_kernel(cell, worker, meta):
    chunk = 96
    for start in range(0, cell.shape[0], chunk):
        values = cell[pl.ds(start, chunk), :]
        target = iota(values.shape, 1) & (WINDOW - 1)
        count = jnp.zeros_like(values)
        for step in (64, 32, 16, 8, 4, 2, 1):
            probe = lane_pick(values, count + (step - 1))
            count = jnp.where(probe <= target, count + step, count)
        count = jnp.where(lane_pick(values, count) <= target, count + 1, count)
        odd = worker[pl.ds(start, chunk), :] & 1
        meta[pl.ds(start, chunk), :] = count + (odd << 8)


def segment_plan(cell, worker):
    return pl.pallas_call(
        segment_plan_kernel,
        out_shape=jax.ShapeDtypeStruct(cell.shape, jnp.int32),
        compiler_params=pltpu.CompilerParams(vmem_limit_bytes=VMEM_LIMIT),
        cost_estimate=pl.CostEstimate(flops=10**8, bytes_accessed=1 * MIB, transcendentals=0),
        name="segment_plan",
    )(cell, worker)


def land_kernel(
    pairs, slots, first_rows, arrived, cell, meta, area, water, cap, soil_in, porosity_in,
    drainage_in, _, __, soil_out, canopy_new, sums_out, soil, porosity, drainage, fetched,
    flows, surfaces, evaps, ready, written,
):
    layers, rows = soil.shape[:2]
    groups = written.shape[0]
    depth = layers // groups
    chunk = 48
    block = 96
    arrays = ((soil_in, soil), (porosity_in, porosity), (drainage_in, drainage))

    def reads(group):
        part = pl.ds(group * depth, depth)
        return [
            pltpu.make_async_copy(source.at[part], target.at[part], ready.at[group, i])
            for i, (source, target) in enumerate(arrays)
        ]

    def write(group):
        part = pl.ds(group * depth, depth)
        return pltpu.make_async_copy(soil.at[part], soil_out.at[part], written.at[group])

    def canopy(start):
        part = pl.ds(start, chunk)
        index = cell[part, :]
        one = fetched[pl.ds(2 * start, chunk, stride=2), :]
        two = fetched[pl.ds(2 * start + 1, chunk, stride=2), :]
        odd = meta[part, :] >> 8
        loss = jnp.where(odd == 1, two, one)
        rain = lane_pick(jnp.where(odd == 1, one, two), index + odd * WINDOW)
        demand = lane_pick(loss, index)
        limit = lane_pick(loss, index + WINDOW)
        wetted = water[part, :] + rain
        retained = jnp.minimum(wetted, cap[part, :])
        canopy_loss = jnp.minimum(demand, retained)
        canopy_new[part, :] = retained - canopy_loss
        flows[part, :] = jnp.maximum(wetted - cap[part, :], 0.0)
        surfaces[part, :] = jnp.minimum(limit, demand - canopy_loss)
        evaps[part, :] = canopy_loss

    def cascade(group, start):
        part = pl.ds(start, chunk)
        flowing = flows[part, :]
        surface = jnp.zeros_like(flowing) if group == 0 else surfaces[part, :]
        for layer in range(group * depth, (group + 1) * depth):
            filled = soil[layer, part, :] + flowing
            excess = jnp.maximum(filled - porosity[layer, part, :], 0.0)
            surface = surface + excess
            filled = filled - excess
            flowing = drainage[layer, part, :] * filled
            middle = filled - flowing
            if layer == 0:
                soil_loss = jnp.minimum(surfaces[part, :], 0.5 * middle)
                middle = middle - soil_loss
                evaps[part, :] = area[part, :] * (evaps[part, :] + soil_loss)
            soil[layer, part, :] = middle
        if group < groups - 1:
            flows[part, :] = flowing
            surfaces[part, :] = surface
        else:
            flows[part, :] = area[part, :] * (surface + flowing)

    def reached(values, part):
        shape = (2 * LANES, LANES)
        upto = onehot((iota(shape, 0) & 127) <= iota(shape, 1))
        count = meta[part, :] & 255
        sums = matmul(jnp.concatenate(halves(values[part, :]), axis=1), upto)
        return jnp.where(count > 0, lane_pick(sums, jnp.maximum(count - 1, 0)), 0.0)

    def hand_back(start):
        part = pl.ds(start, block)
        here = iota((block, LANES), 1)
        sums = jnp.where(here < WINDOW, reached(flows, part), evaps[part, :])
        before = jnp.where((here & (WINDOW - 1)) == 0, 0.0, pltpu.roll(sums, 1, 1))
        surfaces[part, :] = sums - before
        for i in range(start, start + block):
            sums_out[pl.ds(slots[i], 1), :] = surfaces[pl.ds(i, 1), :]

    for group in range(groups):
        for copy in reads(group):
            copy.start()
    sums_out[...] = jnp.zeros_like(sums_out)
    for i in range(rows):
        fetched[pl.ds(2 * i, 2), :] = arrived[pl.ds(first_rows[i], 2, stride=pairs), :]
    for start in range(0, rows, chunk):
        canopy(start)
    for group in range(groups):
        for copy in reads(group):
            copy.wait()
        for start in range(0, rows, chunk):
            cascade(group, start)
        write(group).start()
        if group == min(1, groups - 1):
            for start in range(0, rows, block):
                evaps[pl.ds(start, block), :] = reached(evaps, pl.ds(start, block))
    for start in range(0, rows, block):
        hand_back(start)
    for group in range(groups):
        write(group).wait()


def land_step(
    sums_shape, pairs, slots, first_rows, arrived, cell, meta, area, water, cap, soil, porosity,
    drainage, after,
):
    layers, rows = soil.shape[:2]
    groups = 5 if layers % 5 == 0 else 1
    near = pl.BlockSpec(memory_space=pltpu.VMEM)
    far = pl.BlockSpec(memory_space=pltpu.HBM)
    return pl.pallas_call(
        functools.partial(land_kernel, pairs),
        in_specs=[pl.BlockSpec(memory_space=pltpu.SMEM)] * 2 + [near] * 6 + [far] * 3
        + [pl.BlockSpec(memory_space=pl.ANY)] * 2,
        out_specs=[far, near, near],
        scratch_shapes=[pltpu.VMEM(soil.shape, jnp.float32)] * 3
        + [pltpu.VMEM((2 * rows, LANES), jnp.float32)]
        + [pltpu.VMEM((rows, LANES), jnp.float32)] * 3
        + [pltpu.SemaphoreType.DMA((groups, 3)), pltpu.SemaphoreType.DMA((groups,))],
        out_shape=(
            jax.ShapeDtypeStruct(soil.shape, jnp.float32),
            jax.ShapeDtypeStruct((rows, LANES), jnp.float32),
            jax.ShapeDtypeStruct(sums_shape, jnp.float32),
        ),
        compiler_params=pltpu.CompilerParams(vmem_limit_bytes=VMEM_LIMIT),
        cost_estimate=pl.CostEstimate(flops=10**8, bytes_accessed=20 * MIB, transcendentals=0),
        name="land_layers",
    )(
        slots, first_rows, arrived, cell, meta, area, water, cap,
        in_hbm(soil), in_hbm(porosity), in_hbm(drainage), *after,
    )


def halo_parts(value, axis, dim, width):
    count, length = (lax.axis_size(axis), value.shape[dim])
    up = [(i, i + 1) for i in range(count - 1)]
    down = [(j, i) for i, j in up]
    last = lax.slice_in_dim(value, length - width, length, axis=dim)
    initial = lax.slice_in_dim(value, 0, width, axis=dim)
    return lax.ppermute(last, axis, up), lax.ppermute(initial, axis, down)


def edge_columns_kernel(tall, _, first, last):
    arrays, height, width = tall.shape
    for number in range(arrays):
        values = tall[number]
        values = jnp.concatenate([values, jnp.zeros((LANES - height, width), jnp.float32)], axis=0)
        columns = jnp.transpose(values)
        part = pl.ds(number * ITERS, ITERS)
        first[part, :] = columns[:ITERS]
        last[part, :] = columns[width - ITERS :]


def edge_columns(tall, after):
    shape = jax.ShapeDtypeStruct((2 * ITERS, LANES), jnp.float32)
    return pl.pallas_call(
        edge_columns_kernel,
        in_specs=[pl.BlockSpec(memory_space=pltpu.VMEM), pl.BlockSpec(memory_space=pl.ANY)],
        out_shape=(shape, shape),
        compiler_params=pltpu.CompilerParams(vmem_limit_bytes=VMEM_LIMIT),
        cost_estimate=pl.CostEstimate(flops=10**6, bytes_accessed=10**5, transcendentals=0),
        name="edge_columns",
    )(tall, after)


def extended(own, strip):
    height = own.shape[0]

    def column_strip(right):
        middle, above, below = strip(0, right), strip(-1, right), strip(1, right)
        return jnp.concatenate(
            [
                middle[:, :height],
                below[:, :ITERS],
                above[:, height - ITERS : height],
                jnp.zeros((ITERS, LANES - height - 2 * ITERS), jnp.float32),
            ],
            axis=1,
        )

    gap = jnp.zeros((LANES - 2 * ITERS, LANES), jnp.float32)
    sides = jnp.concatenate([column_strip(1), gap, column_strip(-1)], axis=0)
    sides = jnp.transpose(sides)[: height + 2 * ITERS]
    tall = jnp.concatenate([own, strip(1, 0), strip(-1, 0)], axis=0)
    return jnp.concatenate([tall, sides], axis=1)


def neighbour(down, right):
    row, column = lax.axis_index("region") + down, lax.axis_index("col") + right
    there = (row >= 0) & (row < lax.axis_size("region"))
    there &= (column >= 0) & (column < lax.axis_size("col"))
    return jnp.where(there, row * lax.axis_size("col") + column, 0), jnp.where(there, 1.0, 0.0)


def static_halo_kernel(tall, before, after, out):
    height, width = tall.shape[1:]
    gap = jnp.zeros((LANES - 2 * ITERS, LANES), jnp.float32)
    for number in range(2):
        part = pl.ds(number * ITERS, ITERS)
        sides = jnp.transpose(jnp.concatenate([after[part, :], gap, before[part, :]], axis=0))
        out[number, :, :width] = tall[number]
        out[number, :, width:] = sides[:height]


def static_halo(tall, before, after):
    arrays, height, width = tall.shape
    return pl.pallas_call(
        static_halo_kernel,
        out_shape=jax.ShapeDtypeStruct((arrays, height, width + LANES), jnp.float32),
        compiler_params=pltpu.CompilerParams(vmem_limit_bytes=VMEM_LIMIT),
        cost_estimate=pl.CostEstimate(flops=10**6, bytes_accessed=10**6, transcendentals=0),
        name="static_halo",
    )(tall, before, after)


def river_kernel(state, strips, fixed, out):
    height, width = state.shape

    def strip(down, right):
        device, there = neighbour(down, right)
        return strips[pl.ds(device * ITERS, ITERS), :] * there

    storage = extended(state[...], strip)
    rate = fixed[0]
    code = fixed[1]
    rows, cols = storage.shape
    for _ in range(ITERS):
        outflow = rate * storage
        inflow = jnp.zeros_like(storage)
        for col_step in (-1, 0, 1):
            column = jnp.zeros_like(storage)
            for bit, (row_step, step) in enumerate(directions):
                if step != col_step:
                    continue
                leaving = jnp.where(code == float(1 << bit), outflow, 0.0)
                if row_step:
                    leaving = pltpu.roll(leaving, row_step % rows, 0)
                column = column + leaving
            if col_step:
                column = pltpu.roll(column, col_step % cols, 1)
            inflow = inflow + column
        storage = storage - outflow + inflow
    out[...] = storage[:height, :width]


def river(state, strips, fixed):
    return pl.pallas_call(
        river_kernel,
        out_shape=jax.ShapeDtypeStruct(state.shape, jnp.float32),
        compiler_params=pltpu.CompilerParams(vmem_limit_bytes=VMEM_LIMIT),
        cost_estimate=pl.CostEstimate(flops=10**7, bytes_accessed=1 * MIB, transcendentals=0),
        name="river_steps",
    )(state, strips, fixed)


def exchange(value):
    return lax.all_to_all(value, axes, split_axis=0, concat_axis=0, tiled=True)


def shards(
    forcing,
    river_storage,
    river_rate,
    flow_code,
    home_slot,
    home_offset,
    worker_list,
    patch_cell,
    patch_area,
    canopy_water,
    canopy_cap,
    soil_water,
    porosity,
    drainage,
):
    homes = lax.axis_size("region") * lax.axis_size("col")
    capacity = home_slot.shape[1] // homes
    grid_rows, grid_cols = river_storage.shape
    lane_rows = grid_rows * grid_cols // LANES
    outgoing = pack(
        homes, capacity, home_slot, home_offset, forcing.reshape(3, lane_rows, LANES)
    )
    arrived = exchange(outgoing)
    home = worker_list // capacity
    position = worker_list - home * capacity
    pairs = capacity // 2
    first_rows = home * (3 * pairs) + position // 2 + position % 2 * pairs
    meta = segment_plan(patch_cell, worker_list[:, None])
    fixed = jnp.stack([river_rate, flow_code.astype(jnp.float32)])
    above, below = halo_parts(fixed, "region", 1, ITERS)
    soil_new, canopy_new, sums = land_step(
        (homes * capacity, LANES), pairs, worker_list, first_rows, arrived, patch_cell, meta,
        patch_area, canopy_water, canopy_cap, soil_water, porosity, drainage, (above, below),
    )
    returned = exchange(sums)
    code, place = unpack_plan(homes, capacity, lane_rows, home_slot, home_offset)
    fixed = jnp.concatenate([fixed, below, above], axis=1)
    initial, last = edge_columns(fixed, sums)
    count = lax.axis_size("col")
    before = lax.ppermute(last, "col", [(i, i + 1) for i in range(count - 1)])
    after = lax.ppermute(initial, "col", [(i + 1, i) for i in range(count - 1)])
    fixed = static_halo(fixed, before, after)
    cell_runoff, storage, strips = unpack_runoff(
        homes, returned, code, place, river_storage.reshape(lane_rows, LANES), fixed
    )
    cell_evap = unpack_evap(returned, code, place)
    river_new = river(storage.reshape(river_storage.shape), exchange(strips), fixed)
    return (
        soil_new,
        canopy_new,
        cell_runoff.reshape(river_storage.shape),
        cell_evap.reshape(river_storage.shape),
        river_new,
    )


def solution(mesh):
    placed = (
        P(None, "region", "col"),
        P("region", "col"),
        P("region", "col"),
        P("region", "col"),
        P(("region", "col"), None),
        P(("region", "col"), None),
        P(("region", "col")),
        P(("region", "col"), None),
        P(("region", "col"), None),
        P(("region", "col"), None),
        P(("region", "col"), None),
        P(None, ("region", "col"), None),
        P(None, ("region", "col"), None),
        P(None, ("region", "col"), None),
    )
    return jax.shard_map(
        shards,
        mesh=mesh,
        in_specs=placed,
        out_specs=(
            P(None, ("region", "col"), None),
            P(("region", "col"), None),
            P("region", "col"),
            P("region", "col"),
            P("region", "col"),
        ),
        check_vma=False,
    )
```

profile of v0, /device:TPU:0, one launch (start us, length us, event | category | flops | bytes accessed | tf_op | source)
XLA Modules:
  0.0 73.2 jit_solution(11593244824847139806)
XLA Ops:
  0.6 0.0 copy-start.9
  0.6 0.0 copy-start.8
  0.7 0.0 copy-start.4
  0.7 0.0 copy-start
  0.7 0.0 copy-start.1
  0.7 0.0 copy-start.2
  0.7 0.0 copy-start.3
  0.7 3.6 %pack_forcing.1 = f32[1536,128]{1,0:T(8,128)} custom-call(s32[1,1024]{1,0:T(1,128)} %slot.1, s32[1,1024]{1,0:T(1,128)} %offset.1, f32[3,64,128]{2,1,0:T(8,128)} %forcing_in.1), custom_call_target="tpu_custom_call" | custom-call | flops 1000000000 | bytes 2097152 | tf_op jit(solution)/shard_map/pack_forcing/pallas_call | solution.py:166
  4.3 7.3 %all-to-all-start = ((f32[32,48,128]{2,1,0:T(8,128)}), f32[32,48,128]{2,1,0:T(8,128)S(1)}, u32[]{:S(2)}, u32[]{:S(2)}) async-start(f32[32,48,128]{2,1,0:T(8,128)} %bitcast), calls=%async_computation | async-start | bytes 1572864 | tf_op jit(solution)/shard_map/all_to_all | solution.py:565
  11.6 0.0 copy-done.9
  11.7 0.0 copy-done.8
  11.7 3.7 %collective-permute-start = (f32[2,4,128]{2,1,0:T(4,128)S(1)}, f32[2,4,128]{2,1,0:T(4,128)S(1)}, u32[]{:S(2)}, u32[]{:S(2)}) collective-permute-start(f32[2,4,128]{2,1,0:T(4,128)S(1)} %get-tuple-element.26), channel_id=1, source_target_pairs={{0,8},{8,16},{16,24},{1,9},{9,17},{17,25},{2,10},{10,18},{18,26},{... | collective-permute-start | bytes 12296 | tf_op jit(solution)/shard_map/ppermute | solution.py:448
  15.4 1.3 %collective-permute-start.1 = (f32[2,4,128]{2,1,0:T(4,128)S(1)}, f32[2,4,128]{2,1,0:T(4,128)S(1)}, u32[]{:S(2)}, u32[]{:S(2)}) collective-permute-start(f32[2,4,128]{2,1,0:T(4,128)S(1)} %get-tuple-element.25), channel_id=1, source_target_pairs={{8,0},{16,8},{24,16},{9,1},{17,9},{25,17},{10,2},{18,10},{26,18},{... | collective-permute-start | bytes 12296 | tf_op jit(solution)/shard_map/ppermute | solution.py:448
  16.7 0.0 copy-done.4
  16.7 0.1 copy.19.worker
  16.8 0.0 copy-done
  16.9 1.9 %segment_plan.1.meta = s32[480,128]{1,0:T(8,128)S(1)} custom-call(s32[480,128]{1,0:T(8,128)S(1)} %copy-done, s32[480,1]{1,0:T(8,128)S(1)} %copy.19.worker), custom_call_target="tpu_custom_call" | custom-call | flops 100000000 | bytes 1048576 | tf_op jit(solution)/shard_map/segment_plan/pallas_call | solution.py:300
  18.8 6.3 %collective-permute-done._ = f32[2,4,128]{2,1,0:T(4,128)S(1)} collective-permute-done((f32[2,4,128]{2,1,0:T(4,128)S(1)}, f32[2,4,128]{2,1,0:T(4,128)S(1)}, u32[]{:S(2)}, u32[]{:S(2)}) %collective-permute-start) | collective-permute-done | bytes 4128 | tf_op jit(solution)/shard_map/ppermute | solution.py:448
  25.1 0.0 collective-permute-done.1.__
  25.1 7.2 %all-to-all-done = f32[32,48,128]{2,1,0:T(8,128)S(1)} async-done(((f32[32,48,128]{2,1,0:T(8,128)}), f32[32,48,128]{2,1,0:T(8,128)S(1)}, u32[]{:S(2)}, u32[]{:S(2)}) %all-to-all-start) | async-done | bytes 786464 | tf_op jit(solution)/shard_map/all_to_all | solution.py:565
  32.3 0.0 copy-done.1
  32.3 0.0 copy-done.2
  32.3 0.0 copy-done.3
  32.3 0.0 copy-start.6
  32.3 0.0 copy-start.7
  32.3 8.6 %land_layers.1 = (f32[15,480,128]{2,1,0:T(8,128)}, f32[480,128]{1,0:T(8,128)}, f32[1024,128]{1,0:T(8,128)}) custom-call(s32[480]{0:T(512)S(1)} %copy-done.4, s32[480]{0:T(512)S(1)} %fusion.2.first_rows, f32[1536,128]{1,0:T(8,128)S(1)} %bitcast.10, s32[480,128]{1,0:T(8,128)S(1)} %copy-done, s32[480,128]{1,0:T(8,128)S(1)} %segment_plan.1.meta, ...), custom_call_target="tpu_custom_call" | custom-call | flops 100000000 | bytes 20971520 | tf_op jit(solution)/shard_map/land_layers/pallas_call | solution.py:419
  40.9 0.0 copy-start.5
  40.9 3.6 %all-to-all-start.1 = ((f32[32,32,128]{2,1,0:T(8,128)}), f32[32,32,128]{2,1,0:T(8,128)S(1)}, u32[]{:S(2)}, u32[]{:S(2)}) async-start(f32[32,32,128]{2,1,0:T(8,128)} %bitcast.5), calls=%async_computation.1 | async-start | bytes 1048576 | tf_op jit(solution)/shard_map/all_to_all | solution.py:565
  44.6 0.1 edge_columns.1
  44.7 2.2 %collective-permute-start.2 = (f32[8,128]{1,0:T(8,128)S(1)}, f32[8,128]{1,0:T(8,128)S(1)}, u32[]{:S(2)}, u32[]{:S(2)}) collective-permute-start(f32[8,128]{1,0:T(8,128)S(1)} %get-tuple-element.20), channel_id=1, source_target_pairs={{0,1},{1,2},{2,3},{3,4},{4,5},{5,6},{6,7},{8,9},{9,10},{10,11},{11... | collective-permute-start | bytes 12296 | tf_op jit(solution)/shard_map/ppermute | solution.py:608
  46.8 1.3 %collective-permute-start.3 = (f32[8,128]{1,0:T(8,128)S(1)}, f32[8,128]{1,0:T(8,128)S(1)}, u32[]{:S(2)}, u32[]{:S(2)}) collective-permute-start(f32[8,128]{1,0:T(8,128)S(1)} %get-tuple-element.21), channel_id=1, source_target_pairs={{1,0},{2,1},{3,2},{4,3},{5,4},{6,5},{7,6},{9,8},{10,9},{11,10},{12... | collective-permute-start | bytes 12296 | tf_op jit(solution)/shard_map/ppermute | solution.py:609
  48.1 0.0 copy-done.6
  48.1 0.0 copy-done.7
  48.2 0.7 unpack_plan.1
  48.8 0.0 collective-permute-done.2.before
  48.8 2.2 %collective-permute-done.3.after = f32[8,128]{1,0:T(8,128)S(1)} collective-permute-done((f32[8,128]{1,0:T(8,128)S(1)}, f32[8,128]{1,0:T(8,128)S(1)}, u32[]{:S(2)}, u32[]{:S(2)}) %collective-permute-start.3) | collective-permute-done | bytes 4128 | tf_op jit(solution)/shard_map/ppermute | solution.py:609
  51.0 0.1 static_halo.1._.fixed
  51.1 9.0 %all-to-all-done.1 = f32[32,32,128]{2,1,0:T(8,128)S(1)} async-done(((f32[32,32,128]{2,1,0:T(8,128)}), f32[32,32,128]{2,1,0:T(8,128)S(1)}, u32[]{:S(2)}, u32[]{:S(2)}) %all-to-all-start.1) | async-done | bytes 524320 | tf_op jit(solution)/shard_map/all_to_all | solution.py:565
  60.1 0.0 copy-done.5
  60.1 1.4 %unpack_runoff.1 = (f32[64,128]{1,0:T(8,128)}, f32[64,128]{1,0:T(8,128)S(1)}, f32[128,128]{1,0:T(8,128)}) custom-call(f32[1024,128]{1,0:T(8,128)S(1)} %bitcast.11, s32[1024,128]{1,0:T(8,128)S(1)} %get-tuple-element.18.code, bf16[64,1024]{1,0:T(8,128)(2,1)S(1)} %get-tuple-element.19.place, f32[64,128]{1,0:T(8,128)S(1)} %copy-done.5, ...), custom_call_target="tpu_custom_call" | custom-call | flops 1000000000 | bytes 1048576 | tf_op jit(solution)/shard_map/unpack_runoff/pallas_call | solution.py:261
  61.5 3.1 %all-to-all-start.2 = ((f32[32,4,128]{2,1,0:T(4,128)}), f32[32,4,128]{2,1,0:T(4,128)S(1)}, u32[]{:S(2)}, u32[]{:S(2)}) async-start(f32[32,4,128]{2,1,0:T(4,128)} %bitcast.7), calls=%async_computation.2 | async-start | bytes 131072 | tf_op jit(solution)/shard_map/all_to_all | solution.py:565
  64.5 1.2 %unpack_evap.1 = f32[64,128]{1,0:T(8,128)} custom-call(f32[1024,128]{1,0:T(8,128)S(1)} %bitcast.12, s32[1024,128]{1,0:T(8,128)S(1)} %get-tuple-element.18.code, bf16[64,1024]{1,0:T(8,128)(2,1)S(1)} %get-tuple-element.19.place), custom_call_target="tpu_custom_call" | custom-call | flops 1000000000 | bytes 1048576 | tf_op jit(solution)/shard_map/unpack_evap/pallas_call | solution.py:276
  65.8 6.2 %all-to-all-done.2 = f32[32,4,128]{2,1,0:T(4,128)S(1)} async-done(((f32[32,4,128]{2,1,0:T(4,128)}), f32[32,4,128]{2,1,0:T(4,128)S(1)}, u32[]{:S(2)}, u32[]{:S(2)}) %all-to-all-start.2) | async-done | bytes 65568 | tf_op jit(solution)/shard_map/all_to_all | solution.py:565
  71.9 1.2 %river_steps.1 = f32[64,128]{1,0:T(8,128)} custom-call(f32[64,128]{1,0:T(8,128)S(1)} %get-tuple-element.23.state, f32[128,128]{1,0:T(8,128)S(1)} %bitcast.13, f32[2,72,256]{2,1,0:T(8,128)S(1)} %static_halo.1._.fixed), custom_call_target="tpu_custom_call" | custom-call | flops 10000000 | bytes 1048576 | tf_op jit(solution)/shard_map/river_steps/pallas_call | solution.py:555
  (4 shorter events, 0.0 us)
Async XLA Ops:
  0.6 11.0 %copy-start.9 = (s32[64,128]{1,0:T(8,128)S(1)}, s32[64,128]{1,0:T(8,128)}, u32[]{:S(2)}) copy-start(s32[64,128]{1,0:T(8,128)} %param.17) | copy-start | bytes 98308
  0.6 11.0 %copy-start.8 = (f32[64,128]{1,0:T(8,128)S(1)}, f32[64,128]{1,0:T(8,128)}, u32[]{:S(2)}) copy-start(f32[64,128]{1,0:T(8,128)} %param.16) | copy-start | bytes 98308
  0.7 16.0 %copy-start.4 = (s32[480]{0:T(512)S(1)}, s32[480]{0:T(512)}, u32[]{:S(2)}) copy-start(s32[480]{0:T(512)} %slots.1) | copy-start | bytes 5764
  0.7 16.2 %copy-start = (s32[480,128]{1,0:T(8,128)S(1)}, s32[480,128]{1,0:T(8,128)}, u32[]{:S(2)}) copy-start(s32[480,128]{1,0:T(8,128)} %cell.3) | copy-start | bytes 737284
  0.7 31.6 %copy-start.1 = (f32[480,128]{1,0:T(8,128)S(1)}, f32[480,128]{1,0:T(8,128)}, u32[]{:S(2)}) copy-start(f32[480,128]{1,0:T(8,128)} %area.1) | copy-start | bytes 737284
  0.7 31.6 %copy-start.2 = (f32[480,128]{1,0:T(8,128)S(1)}, f32[480,128]{1,0:T(8,128)}, u32[]{:S(2)}) copy-start(f32[480,128]{1,0:T(8,128)} %water.1) | copy-start | bytes 737284
  0.7 31.6 %copy-start.3 = (f32[480,128]{1,0:T(8,128)S(1)}, f32[480,128]{1,0:T(8,128)}, u32[]{:S(2)}) copy-start(f32[480,128]{1,0:T(8,128)} %cap.1) | copy-start | bytes 737284
  4.3 28.0 %all-to-all-start = ((f32[32,48,128]{2,1,0:T(8,128)}), f32[32,48,128]{2,1,0:T(8,128)S(1)}, u32[]{:S(2)}, u32[]{:S(2)}) async-start(f32[32,48,128]{2,1,0:T(8,128)} %bitcast), calls=%async_computation | async-start | bytes 1572864 | tf_op jit(solution)/shard_map/all_to_all | solution.py:565
  11.7 13.4 %collective-permute-start = (f32[2,4,128]{2,1,0:T(4,128)S(1)}, f32[2,4,128]{2,1,0:T(4,128)S(1)}, u32[]{:S(2)}, u32[]{:S(2)}) collective-permute-start(f32[2,4,128]{2,1,0:T(4,128)S(1)} %get-tuple-element.26), channel_id=1, source_target_pairs={{0,8},{8,16},{16,24},{1,9},{9,17},{17,25},{2,10},{10,18},{18,26},{... | collective-permute-start | bytes 12296 | tf_op jit(solution)/shard_map/ppermute | solution.py:448
  15.4 9.7 %collective-permute-start.1 = (f32[2,4,128]{2,1,0:T(4,128)S(1)}, f32[2,4,128]{2,1,0:T(4,128)S(1)}, u32[]{:S(2)}, u32[]{:S(2)}) collective-permute-start(f32[2,4,128]{2,1,0:T(4,128)S(1)} %get-tuple-element.25), channel_id=1, source_target_pairs={{8,0},{16,8},{24,16},{9,1},{17,9},{25,17},{10,2},{18,10},{26,18},{... | collective-permute-start | bytes 12296 | tf_op jit(solution)/shard_map/ppermute | solution.py:448
  32.3 15.8 %copy-start.6 = (s32[1,1024]{1,0:T(1,128)S(1)}, s32[1,1024]{1,0:T(1,128)}, u32[]{:S(2)}) copy-start(s32[1,1024]{1,0:T(1,128)} %slot.1) | copy-start | bytes 12292
  32.3 15.8 %copy-start.7 = (s32[1,1024]{1,0:T(1,128)S(1)}, s32[1,1024]{1,0:T(1,128)}, u32[]{:S(2)}) copy-start(s32[1,1024]{1,0:T(1,128)} %offset.1) | copy-start | bytes 12292
  40.9 19.2 %copy-start.5 = (f32[64,128]{1,0:T(8,128)S(1)}, f32[64,128]{1,0:T(8,128)}, u32[]{:S(2)}) copy-start(f32[64,128]{1,0:T(8,128)} %river.1) | copy-start | bytes 98308
  40.9 19.2 %all-to-all-start.1 = ((f32[32,32,128]{2,1,0:T(8,128)}), f32[32,32,128]{2,1,0:T(8,128)S(1)}, u32[]{:S(2)}, u32[]{:S(2)}) async-start(f32[32,32,128]{2,1,0:T(8,128)} %bitcast.5), calls=%async_computation.1 | async-start | bytes 1048576 | tf_op jit(solution)/shard_map/all_to_all | solution.py:565
  44.7 4.2 %collective-permute-start.2 = (f32[8,128]{1,0:T(8,128)S(1)}, f32[8,128]{1,0:T(8,128)S(1)}, u32[]{:S(2)}, u32[]{:S(2)}) collective-permute-start(f32[8,128]{1,0:T(8,128)S(1)} %get-tuple-element.20), channel_id=1, source_target_pairs={{0,1},{1,2},{2,3},{3,4},{4,5},{5,6},{6,7},{8,9},{9,10},{10,11},{11... | collective-permute-start | bytes 12296 | tf_op jit(solution)/shard_map/ppermute | solution.py:608
  46.8 4.2 %collective-permute-start.3 = (f32[8,128]{1,0:T(8,128)S(1)}, f32[8,128]{1,0:T(8,128)S(1)}, u32[]{:S(2)}, u32[]{:S(2)}) collective-permute-start(f32[8,128]{1,0:T(8,128)S(1)} %get-tuple-element.21), channel_id=1, source_target_pairs={{1,0},{2,1},{3,2},{4,3},{5,4},{6,5},{7,6},{9,8},{10,9},{11,10},{12... | collective-permute-start | bytes 12296 | tf_op jit(solution)/shard_map/ppermute | solution.py:609
  61.5 10.5 %all-to-all-start.2 = ((f32[32,4,128]{2,1,0:T(4,128)}), f32[32,4,128]{2,1,0:T(4,128)S(1)}, u32[]{:S(2)}, u32[]{:S(2)}) async-start(f32[32,4,128]{2,1,0:T(4,128)} %bitcast.7), calls=%async_computation.2 | async-start | bytes 131072 | tf_op jit(solution)/shard_map/all_to_all | solution.py:565
where the time goes:
time: 73.6 us; the launch traced here: 73.2 us
  waiting for transfers between devices  30.9 us (42%)
  starting transfers between devices  22.4 us (30%)
  Pallas kernels  18.7 us (25%)
  between operations  0.91 us (1%)
    all_to_all x3, waiting for transfers between devices, exchange(): return lax.all_to_all(value, axes, split_axis=0, concat_axis=0, tiled=True)  22.4 us
    all_to_all x3, starting transfers between devices, exchange(): return lax.all_to_all(value, axes, split_axis=0, concat_axis=0, tiled=True)  14 us
    pallas_call x1, Pallas kernels, land_step(): pl.pallas_call(functools.partial(land_kernel, pairs), in_specs=[pl.BlockS...  8.58 us
    ppermute x2, waiting for transfers between devices, halo_parts(): return (lax.ppermute(last, axis, up), lax.ppermute(initial, axis, down))  6.33 us
    ppermute x2, starting transfers between devices, halo_parts(): return (lax.ppermute(last, axis, up), lax.ppermute(initial, axis, down))  4.97 us
    pallas_call x1, Pallas kernels, pack(): pl.pallas_call(functools.partial(pack_kernel, homes, capacity), in_specs=...  3.61 us
    ppermute x1, waiting for transfers between devices, shards(): after = lax.ppermute(initial, 'col', [(i + 1, i) for i in range(count - 1)])  2.2 us
    ppermute x1, starting transfers between devices, shards(): before = lax.ppermute(last, 'col', [(i, i + 1) for i in range(count - 1)])  2.17 us
  transfers between devices with their start and end apart: 7, of which 5 were waited for; matrix products, arithmetic and copies ran while one was open for 0% of the time, Pallas kernels for 5%

commit v1 on v0

--- a/solution.py
+++ b/solution.py
@@ -308,50 +308,58 @@
 
 def land_kernel(
     pairs, slots, first_rows, arrived, cell, meta, area, water, cap, soil_in, porosity_in,
-    drainage_in, _, __, soil_out, canopy_new, sums_out, soil, porosity, drainage, fetched,
-    flows, surfaces, evaps, ready, written,
+    drainage_in, _, __, soil_out, canopy_new, sums_out, soil, porosity, drainage, soil_new,
+    fetched, runoffs, evaps, sums, ready, written,
 ):
     layers, rows = soil.shape[:2]
-    groups = written.shape[0]
-    depth = layers // groups
-    chunk = 48
-    block = 96
+    steps = written.shape[0]
+    block = rows // steps
+    chunk = block // 2
+    ahead = 2
     arrays = ((soil_in, soil), (porosity_in, porosity), (drainage_in, drainage))
 
-    def reads(group):
-        part = pl.ds(group * depth, depth)
+    def part_of(step):
+        return pl.ds(pl.multiple_of(step * block, block), block)
+
+    def reads(step):
         return [
-            pltpu.make_async_copy(source.at[part], target.at[part], ready.at[group, i])
+            pltpu.make_async_copy(
+                source.at[:, part_of(step), :], target.at[:, part_of(step), :], ready.at[step, i]
+            )
             for i, (source, target) in enumerate(arrays)
         ]
 
-    def write(group):
-        part = pl.ds(group * depth, depth)
-        return pltpu.make_async_copy(soil.at[part], soil_out.at[part], written.at[group])
-
-    def canopy(start):
-        part = pl.ds(start, chunk)
+    def start_reads(step):
+        for copy in reads(step):
+            copy.start()
+
+    def write(step):
+        return pltpu.make_async_copy(
+            soil_new.at[:, part_of(step), :], soil_out.at[:, part_of(step), :], written.at[step]
+        )
+
+    def fetch(step):
+        for i in range(block):
+            row = step * block + i
+            fetched[pl.ds(2 * i, 2), :] = arrived[pl.ds(first_rows[row], 2, stride=pairs), :]
+
+    def cascade(step, inner):
+        part = pl.ds(pl.multiple_of(step * block + inner, chunk), chunk)
         index = cell[part, :]
-        one = fetched[pl.ds(2 * start, chunk, stride=2), :]
-        two = fetched[pl.ds(2 * start + 1, chunk, stride=2), :]
+        one = fetched[pl.ds(2 * inner, chunk, stride=2), :]
+        two = fetched[pl.ds(2 * inner + 1, chunk, stride=2), :]
         odd = meta[part, :] >> 8
         loss = jnp.where(odd == 1, two, one)
         rain = lane_pick(jnp.where(odd == 1, one, two), index + odd * WINDOW)
         demand = lane_pick(loss, index)
         limit = lane_pick(loss, index + WINDOW)
         wetted = water[part, :] + rain
+        flowing = jnp.maximum(wetted - cap[part, :], 0.0)
         retained = jnp.minimum(wetted, cap[part, :])
         canopy_loss = jnp.minimum(demand, retained)
         canopy_new[part, :] = retained - canopy_loss
-        flows[part, :] = jnp.maximum(wetted - cap[part, :], 0.0)
-        surfaces[part, :] = jnp.minimum(limit, demand - canopy_loss)
-        evaps[part, :] = canopy_loss
-
-    def cascade(group, start):
-        part = pl.ds(start, chunk)
-        flowing = flows[part, :]
-        surface = jnp.zeros_like(flowing) if group == 0 else surfaces[part, :]
-        for layer in range(group * depth, (group + 1) * depth):
+        surface = jnp.zeros_like(flowing)
+        for layer in range(layers):
             filled = soil[layer, part, :] + flowing
             excess = jnp.maximum(filled - porosity[layer, part, :], 0.0)
             surface = surface + excess
@@ -359,53 +367,54 @@
             flowing = drainage[layer, part, :] * filled
             middle = filled - flowing
             if layer == 0:
-                soil_loss = jnp.minimum(surfaces[part, :], 0.5 * middle)
+                soil_loss = jnp.minimum(jnp.minimum(limit, demand - canopy_loss), 0.5 * middle)
                 middle = middle - soil_loss
-                evaps[part, :] = area[part, :] * (evaps[part, :] + soil_loss)
-            soil[layer, part, :] = middle
-        if group < groups - 1:
-            flows[part, :] = flowing
-            surfaces[part, :] = surface
-        else:
-            flows[part, :] = area[part, :] * (surface + flowing)
-
-    def reached(values, part):
+                evaps[part, :] = area[part, :] * (canopy_loss + soil_loss)
+            soil_new[layer, part, :] = middle
+        runoffs[part, :] = area[part, :] * (surface + flowing)
+
+    def hand_back(step):
+        part = part_of(step)
         shape = (2 * LANES, LANES)
         upto = onehot((iota(shape, 0) & 127) <= iota(shape, 1))
         count = meta[part, :] & 255
-        sums = matmul(jnp.concatenate(halves(values[part, :]), axis=1), upto)
-        return jnp.where(count > 0, lane_pick(sums, jnp.maximum(count - 1, 0)), 0.0)
-
-    def hand_back(start):
-        part = pl.ds(start, block)
+        last = jnp.maximum(count - 1, 0)
         here = iota((block, LANES), 1)
-        sums = jnp.where(here < WINDOW, reached(flows, part), evaps[part, :])
-        before = jnp.where((here & (WINDOW - 1)) == 0, 0.0, pltpu.roll(sums, 1, 1))
-        surfaces[part, :] = sums - before
-        for i in range(start, start + block):
-            sums_out[pl.ds(slots[i], 1), :] = surfaces[pl.ds(i, 1), :]
-
-    for group in range(groups):
-        for copy in reads(group):
-            copy.start()
+        picked = [
+            lane_pick(matmul(jnp.concatenate(halves(value[part, :]), axis=1), upto), last)
+            for value in (runoffs, evaps)
+        ]
+        reached = jnp.where(count > 0, jnp.where(here < WINDOW, *picked), 0.0)
+        before = jnp.where((here & (WINDOW - 1)) == 0, 0.0, pltpu.roll(reached, 1, 1))
+        sums[...] = reached - before
+        for i in range(block):
+            sums_out[pl.ds(slots[step * block + i], 1), :] = sums[pl.ds(i, 1), :]
+
+    for step in range(ahead):
+        start_reads(step)
     sums_out[...] = jnp.zeros_like(sums_out)
-    for i in range(rows):
-        fetched[pl.ds(2 * i, 2), :] = arrived[pl.ds(first_rows[i], 2, stride=pairs), :]
-    for start in range(0, rows, chunk):
-        canopy(start)
-    for group in range(groups):
-        for copy in reads(group):
+    runoffs[pl.ds(0, block), :] = jnp.zeros((block, LANES), jnp.float32)
+    evaps[pl.ds(0, block), :] = jnp.zeros((block, LANES), jnp.float32)
+
+    def round_of(step, carry):
+        fetch(step)
+        for copy in reads(step):
             copy.wait()
-        for start in range(0, rows, chunk):
-            cascade(group, start)
-        write(group).start()
-        if group == min(1, groups - 1):
-            for start in range(0, rows, block):
-                evaps[pl.ds(start, block), :] = reached(evaps, pl.ds(start, block))
-    for start in range(0, rows, block):
-        hand_back(start)
-    for group in range(groups):
-        write(group).wait()
+
+        @pl.when(step + ahead < steps)
+        def _():
+            start_reads(step + ahead)
+
+        hand_back(jnp.maximum(step - 1, 0))
+        for inner in range(0, block, chunk):
+            cascade(step, inner)
+        write(step).start()
+        return carry
+
+    lax.fori_loop(0, steps, round_of, 0)
+    hand_back(steps - 1)
+    for step in range(steps):
+        write(step).wait()
 
 
 def land_step(
@@ -413,7 +422,8 @@
     drainage, after,
 ):
     layers, rows = soil.shape[:2]
-    groups = 5 if layers % 5 == 0 else 1
+    steps = 5
+    block = rows // steps
     near = pl.BlockSpec(memory_space=pltpu.VMEM)
     far = pl.BlockSpec(memory_space=pltpu.HBM)
     return pl.pallas_call(
@@ -421,10 +431,11 @@
         in_specs=[pl.BlockSpec(memory_space=pltpu.SMEM)] * 2 + [near] * 6 + [far] * 3
         + [pl.BlockSpec(memory_space=pl.ANY)] * 2,
         out_specs=[far, near, near],
-        scratch_shapes=[pltpu.VMEM(soil.shape, jnp.float32)] * 3
-        + [pltpu.VMEM((2 * rows, LANES), jnp.float32)]
-        + [pltpu.VMEM((rows, LANES), jnp.float32)] * 3
-        + [pltpu.SemaphoreType.DMA((groups, 3)), pltpu.SemaphoreType.DMA((groups,))],
+        scratch_shapes=[pltpu.VMEM(soil.shape, jnp.float32)] * 4
+        + [pltpu.VMEM((2 * block, LANES), jnp.float32)]
+        + [pltpu.VMEM((rows, LANES), jnp.float32)] * 2
+        + [pltpu.VMEM((block, LANES), jnp.float32)]
+        + [pltpu.SemaphoreType.DMA((steps, 3)), pltpu.SemaphoreType.DMA((steps,))],
         out_shape=(
             jax.ShapeDtypeStruct(soil.shape, jnp.float32),
             jax.ShapeDtypeStruct((rows, LANES), jnp.float32),

time: 73.6 us -> 73.6 us (level)
  no operation moved by 1% of the time
where the time goes in v1:
time: 73.6 us; the launch traced here: 73.1 us
  waiting for transfers between devices  30.9 us (42%)
  starting transfers between devices  22.4 us (30%)
  Pallas kernels  18.6 us (25%)
  between operations  0.91 us (1%)
    all_to_all x3, waiting for transfers between devices, exchange(): return lax.all_to_all(value, axes, split_axis=0, concat_axis=0, tiled=True)  22.4 us
    all_to_all x3, starting transfers between devices, exchange(): return lax.all_to_all(value, axes, split_axis=0, concat_axis=0, tiled=True)  14 us
    pallas_call x1, Pallas kernels, land_step(): pl.pallas_call(functools.partial(land_kernel, pairs), in_specs=[pl.BlockS...  8.53 us
    ppermute x2, waiting for transfers between devices, halo_parts(): return (lax.ppermute(last, axis, up), lax.ppermute(initial, axis, down))  6.33 us
    ppermute x2, starting transfers between devices, halo_parts(): return (lax.ppermute(last, axis, up), lax.ppermute(initial, axis, down))  4.97 us
    pallas_call x1, Pallas kernels, pack(): pl.pallas_call(functools.partial(pack_kernel, homes, capacity), in_specs=...  3.61 us
    ppermute x1, waiting for transfers between devices, shards(): after = lax.ppermute(initial, 'col', [(i + 1, i) for i in range(count - 1)])  2.21 us
    ppermute x1, starting transfers between devices, shards(): before = lax.ppermute(last, 'col', [(i, i + 1) for i in range(count - 1)])  2.17 us
  transfers between devices with their start and end apart: 7, of which 5 were waited for; matrix products, arithmetic and copies ran while one was open for 0% of the time, Pallas kernels for 5%

profile of v1, /device:TPU:0, one launch (start us, length us, event | category | flops | bytes accessed | tf_op | source)
XLA Modules:
  0.0 73.1 jit_solution(17568996503684826900)
XLA Ops:
  0.6 0.0 copy-start.9
  0.6 0.0 copy-start.8
  0.7 0.0 copy-start.4
  0.7 0.0 copy-start
  0.7 0.0 copy-start.1
  0.7 0.0 copy-start.2
  0.7 0.0 copy-start.3
  0.7 3.6 %pack_forcing.1 = f32[1536,128]{1,0:T(8,128)} custom-call(s32[1,1024]{1,0:T(1,128)} %slot.1, s32[1,1024]{1,0:T(1,128)} %offset.1, f32[3,64,128]{2,1,0:T(8,128)} %forcing_in.1), custom_call_target="tpu_custom_call" | custom-call | flops 1000000000 | bytes 2097152 | tf_op jit(solution)/shard_map/pack_forcing/pallas_call | solution.py:166
  4.3 7.3 %all-to-all-start = ((f32[32,48,128]{2,1,0:T(8,128)}), f32[32,48,128]{2,1,0:T(8,128)S(1)}, u32[]{:S(2)}, u32[]{:S(2)}) async-start(f32[32,48,128]{2,1,0:T(8,128)} %bitcast), calls=%async_computation | async-start | bytes 1572864 | tf_op jit(solution)/shard_map/all_to_all | solution.py:576
  11.6 0.0 copy-done.9
  11.7 0.0 copy-done.8
  11.7 3.7 %collective-permute-start = (f32[2,4,128]{2,1,0:T(4,128)S(1)}, f32[2,4,128]{2,1,0:T(4,128)S(1)}, u32[]{:S(2)}, u32[]{:S(2)}) collective-permute-start(f32[2,4,128]{2,1,0:T(4,128)S(1)} %get-tuple-element.26), channel_id=1, source_target_pairs={{0,8},{8,16},{16,24},{1,9},{9,17},{17,25},{2,10},{10,18},{18,26},{... | collective-permute-start | bytes 12296 | tf_op jit(solution)/shard_map/ppermute | solution.py:459
  15.4 1.3 %collective-permute-start.1 = (f32[2,4,128]{2,1,0:T(4,128)S(1)}, f32[2,4,128]{2,1,0:T(4,128)S(1)}, u32[]{:S(2)}, u32[]{:S(2)}) collective-permute-start(f32[2,4,128]{2,1,0:T(4,128)S(1)} %get-tuple-element.25), channel_id=1, source_target_pairs={{8,0},{16,8},{24,16},{9,1},{17,9},{25,17},{10,2},{18,10},{26,18},{... | collective-permute-start | bytes 12296 | tf_op jit(solution)/shard_map/ppermute | solution.py:459
  16.7 0.0 copy-done.4
  16.7 0.1 copy.19.worker
  16.8 0.0 copy-done
  16.9 1.9 %segment_plan.1.meta = s32[480,128]{1,0:T(8,128)S(1)} custom-call(s32[480,128]{1,0:T(8,128)S(1)} %copy-done, s32[480,1]{1,0:T(8,128)S(1)} %copy.19.worker), custom_call_target="tpu_custom_call" | custom-call | flops 100000000 | bytes 1048576 | tf_op jit(solution)/shard_map/segment_plan/pallas_call | solution.py:300
  18.8 6.3 %collective-permute-done._ = f32[2,4,128]{2,1,0:T(4,128)S(1)} collective-permute-done((f32[2,4,128]{2,1,0:T(4,128)S(1)}, f32[2,4,128]{2,1,0:T(4,128)S(1)}, u32[]{:S(2)}, u32[]{:S(2)}) %collective-permute-start) | collective-permute-done | bytes 4128 | tf_op jit(solution)/shard_map/ppermute | solution.py:459
  25.1 0.0 collective-permute-done.1.__
  25.1 7.2 %all-to-all-done = f32[32,48,128]{2,1,0:T(8,128)S(1)} async-done(((f32[32,48,128]{2,1,0:T(8,128)}), f32[32,48,128]{2,1,0:T(8,128)S(1)}, u32[]{:S(2)}, u32[]{:S(2)}) %all-to-all-start) | async-done | bytes 786464 | tf_op jit(solution)/shard_map/all_to_all | solution.py:576
  32.3 0.0 copy-done.1
  32.3 0.0 copy-done.2
  32.3 0.0 copy-done.3
  32.3 0.0 copy-start.6
  32.3 0.0 copy-start.7
  32.3 8.5 %land_layers.1 = (f32[15,480,128]{2,1,0:T(8,128)}, f32[480,128]{1,0:T(8,128)}, f32[1024,128]{1,0:T(8,128)}) custom-call(s32[480]{0:T(512)S(1)} %copy-done.4, s32[480]{0:T(512)S(1)} %fusion.2.first_rows, f32[1536,128]{1,0:T(8,128)S(1)} %bitcast.10, s32[480,128]{1,0:T(8,128)S(1)} %copy-done, s32[480,128]{1,0:T(8,128)S(1)} %segment_plan.1.meta, ...), custom_call_target="tpu_custom_call" | custom-call | flops 100000000 | bytes 20971520 | tf_op jit(solution)/shard_map/land_layers/pallas_call | solution.py:429
  40.9 0.0 copy-start.5
  40.9 3.6 %all-to-all-start.1 = ((f32[32,32,128]{2,1,0:T(8,128)}), f32[32,32,128]{2,1,0:T(8,128)S(1)}, u32[]{:S(2)}, u32[]{:S(2)}) async-start(f32[32,32,128]{2,1,0:T(8,128)} %bitcast.5), calls=%async_computation.1 | async-start | bytes 1048576 | tf_op jit(solution)/shard_map/all_to_all | solution.py:576
  44.5 0.1 edge_columns.1
  44.6 2.2 %collective-permute-start.2 = (f32[8,128]{1,0:T(8,128)S(1)}, f32[8,128]{1,0:T(8,128)S(1)}, u32[]{:S(2)}, u32[]{:S(2)}) collective-permute-start(f32[8,128]{1,0:T(8,128)S(1)} %get-tuple-element.20), channel_id=1, source_target_pairs={{0,1},{1,2},{2,3},{3,4},{4,5},{5,6},{6,7},{8,9},{9,10},{10,11},{11... | collective-permute-start | bytes 12296 | tf_op jit(solution)/shard_map/ppermute | solution.py:619
  46.8 1.3 %collective-permute-start.3 = (f32[8,128]{1,0:T(8,128)S(1)}, f32[8,128]{1,0:T(8,128)S(1)}, u32[]{:S(2)}, u32[]{:S(2)}) collective-permute-start(f32[8,128]{1,0:T(8,128)S(1)} %get-tuple-element.21), channel_id=1, source_target_pairs={{1,0},{2,1},{3,2},{4,3},{5,4},{6,5},{7,6},{9,8},{10,9},{11,10},{12... | collective-permute-start | bytes 12296 | tf_op jit(solution)/shard_map/ppermute | solution.py:620
  48.1 0.0 copy-done.6
  48.1 0.0 copy-done.7
  48.1 0.7 unpack_plan.1
  48.8 0.0 collective-permute-done.2.before
  48.8 2.2 %collective-permute-done.3.after = f32[8,128]{1,0:T(8,128)S(1)} collective-permute-done((f32[8,128]{1,0:T(8,128)S(1)}, f32[8,128]{1,0:T(8,128)S(1)}, u32[]{:S(2)}, u32[]{:S(2)}) %collective-permute-start.3) | collective-permute-done | bytes 4128 | tf_op jit(solution)/shard_map/ppermute | solution.py:620
  51.0 0.1 static_halo.1._.fixed
  51.1 9.0 %all-to-all-done.1 = f32[32,32,128]{2,1,0:T(8,128)S(1)} async-done(((f32[32,32,128]{2,1,0:T(8,128)}), f32[32,32,128]{2,1,0:T(8,128)S(1)}, u32[]{:S(2)}, u32[]{:S(2)}) %all-to-all-start.1) | async-done | bytes 524320 | tf_op jit(solution)/shard_map/all_to_all | solution.py:576
  60.1 0.0 copy-done.5
  60.1 1.3 %unpack_runoff.1 = (f32[64,128]{1,0:T(8,128)}, f32[64,128]{1,0:T(8,128)S(1)}, f32[128,128]{1,0:T(8,128)}) custom-call(f32[1024,128]{1,0:T(8,128)S(1)} %bitcast.11, s32[1024,128]{1,0:T(8,128)S(1)} %get-tuple-element.18.code, bf16[64,1024]{1,0:T(8,128)(2,1)S(1)} %get-tuple-element.19.place, f32[64,128]{1,0:T(8,128)S(1)} %copy-done.5, ...), custom_call_target="tpu_custom_call" | custom-call | flops 1000000000 | bytes 1048576 | tf_op jit(solution)/shard_map/unpack_runoff/pallas_call | solution.py:261
  61.4 3.1 %all-to-all-start.2 = ((f32[32,4,128]{2,1,0:T(4,128)}), f32[32,4,128]{2,1,0:T(4,128)S(1)}, u32[]{:S(2)}, u32[]{:S(2)}) async-start(f32[32,4,128]{2,1,0:T(4,128)} %bitcast.7), calls=%async_computation.2 | async-start | bytes 131072 | tf_op jit(solution)/shard_map/all_to_all | solution.py:576
  64.5 1.2 %unpack_evap.1 = f32[64,128]{1,0:T(8,128)} custom-call(f32[1024,128]{1,0:T(8,128)S(1)} %bitcast.12, s32[1024,128]{1,0:T(8,128)S(1)} %get-tuple-element.18.code, bf16[64,1024]{1,0:T(8,128)(2,1)S(1)} %get-tuple-element.19.place), custom_call_target="tpu_custom_call" | custom-call | flops 1000000000 | bytes 1048576 | tf_op jit(solution)/shard_map/unpack_evap/pallas_call | solution.py:276
  65.7 6.2 %all-to-all-done.2 = f32[32,4,128]{2,1,0:T(4,128)S(1)} async-done(((f32[32,4,128]{2,1,0:T(4,128)}), f32[32,4,128]{2,1,0:T(4,128)S(1)}, u32[]{:S(2)}, u32[]{:S(2)}) %all-to-all-start.2) | async-done | bytes 65568 | tf_op jit(solution)/shard_map/all_to_all | solution.py:576
  71.9 1.2 %river_steps.1 = f32[64,128]{1,0:T(8,128)} custom-call(f32[64,128]{1,0:T(8,128)S(1)} %get-tuple-element.23.state, f32[128,128]{1,0:T(8,128)S(1)} %bitcast.13, f32[2,72,256]{2,1,0:T(8,128)S(1)} %static_halo.1._.fixed), custom_call_target="tpu_custom_call" | custom-call | flops 10000000 | bytes 1048576 | tf_op jit(solution)/shard_map/river_steps/pallas_call | solution.py:566
  (4 shorter events, 0.0 us)
Async XLA Ops:
  0.6 11.0 %copy-start.9 = (s32[64,128]{1,0:T(8,128)S(1)}, s32[64,128]{1,0:T(8,128)}, u32[]{:S(2)}) copy-start(s32[64,128]{1,0:T(8,128)} %param.17) | copy-start | bytes 98308
  0.6 11.0 %copy-start.8 = (f32[64,128]{1,0:T(8,128)S(1)}, f32[64,128]{1,0:T(8,128)}, u32[]{:S(2)}) copy-start(f32[64,128]{1,0:T(8,128)} %param.16) | copy-start | bytes 98308
  0.7 16.0 %copy-start.4 = (s32[480]{0:T(512)S(1)}, s32[480]{0:T(512)}, u32[]{:S(2)}) copy-start(s32[480]{0:T(512)} %slots.1) | copy-start | bytes 5764
  0.7 16.2 %copy-start = (s32[480,128]{1,0:T(8,128)S(1)}, s32[480,128]{1,0:T(8,128)}, u32[]{:S(2)}) copy-start(s32[480,128]{1,0:T(8,128)} %cell.3) | copy-start | bytes 737284
  0.7 31.6 %copy-start.1 = (f32[480,128]{1,0:T(8,128)S(1)}, f32[480,128]{1,0:T(8,128)}, u32[]{:S(2)}) copy-start(f32[480,128]{1,0:T(8,128)} %area.1) | copy-start | bytes 737284
  0.7 31.6 %copy-start.2 = (f32[480,128]{1,0:T(8,128)S(1)}, f32[480,128]{1,0:T(8,128)}, u32[]{:S(2)}) copy-start(f32[480,128]{1,0:T(8,128)} %water.1) | copy-start | bytes 737284
  0.7 31.6 %copy-start.3 = (f32[480,128]{1,0:T(8,128)S(1)}, f32[480,128]{1,0:T(8,128)}, u32[]{:S(2)}) copy-start(f32[480,128]{1,0:T(8,128)} %cap.1) | copy-start | bytes 737284
  4.3 28.0 %all-to-all-start = ((f32[32,48,128]{2,1,0:T(8,128)}), f32[32,48,128]{2,1,0:T(8,128)S(1)}, u32[]{:S(2)}, u32[]{:S(2)}) async-start(f32[32,48,128]{2,1,0:T(8,128)} %bitcast), calls=%async_computation | async-start | bytes 1572864 | tf_op jit(solution)/shard_map/all_to_all | solution.py:576
  11.7 13.4 %collective-permute-start = (f32[2,4,128]{2,1,0:T(4,128)S(1)}, f32[2,4,128]{2,1,0:T(4,128)S(1)}, u32[]{:S(2)}, u32[]{:S(2)}) collective-permute-start(f32[2,4,128]{2,1,0:T(4,128)S(1)} %get-tuple-element.26), channel_id=1, source_target_pairs={{0,8},{8,16},{16,24},{1,9},{9,17},{17,25},{2,10},{10,18},{18,26},{... | collective-permute-start | bytes 12296 | tf_op jit(solution)/shard_map/ppermute | solution.py:459
  15.4 9.7 %collective-permute-start.1 = (f32[2,4,128]{2,1,0:T(4,128)S(1)}, f32[2,4,128]{2,1,0:T(4,128)S(1)}, u32[]{:S(2)}, u32[]{:S(2)}) collective-permute-start(f32[2,4,128]{2,1,0:T(4,128)S(1)} %get-tuple-element.25), channel_id=1, source_target_pairs={{8,0},{16,8},{24,16},{9,1},{17,9},{25,17},{10,2},{18,10},{26,18},{... | collective-permute-start | bytes 12296 | tf_op jit(solution)/shard_map/ppermute | solution.py:459
  32.3 15.8 %copy-start.6 = (s32[1,1024]{1,0:T(1,128)S(1)}, s32[1,1024]{1,0:T(1,128)}, u32[]{:S(2)}) copy-start(s32[1,1024]{1,0:T(1,128)} %slot.1) | copy-start | bytes 12292
  32.3 15.8 %copy-start.7 = (s32[1,1024]{1,0:T(1,128)S(1)}, s32[1,1024]{1,0:T(1,128)}, u32[]{:S(2)}) copy-start(s32[1,1024]{1,0:T(1,128)} %offset.1) | copy-start | bytes 12292
  40.9 19.2 %copy-start.5 = (f32[64,128]{1,0:T(8,128)S(1)}, f32[64,128]{1,0:T(8,128)}, u32[]{:S(2)}) copy-start(f32[64,128]{1,0:T(8,128)} %river.1) | copy-start | bytes 98308
  40.9 19.2 %all-to-all-start.1 = ((f32[32,32,128]{2,1,0:T(8,128)}), f32[32,32,128]{2,1,0:T(8,128)S(1)}, u32[]{:S(2)}, u32[]{:S(2)}) async-start(f32[32,32,128]{2,1,0:T(8,128)} %bitcast.5), calls=%async_computation.1 | async-start | bytes 1048576 | tf_op jit(solution)/shard_map/all_to_all | solution.py:576
  44.6 4.2 %collective-permute-start.2 = (f32[8,128]{1,0:T(8,128)S(1)}, f32[8,128]{1,0:T(8,128)S(1)}, u32[]{:S(2)}, u32[]{:S(2)}) collective-permute-start(f32[8,128]{1,0:T(8,128)S(1)} %get-tuple-element.20), channel_id=1, source_target_pairs={{0,1},{1,2},{2,3},{3,4},{4,5},{5,6},{6,7},{8,9},{9,10},{10,11},{11... | collective-permute-start | bytes 12296 | tf_op jit(solution)/shard_map/ppermute | solution.py:619
  46.8 4.2 %collective-permute-start.3 = (f32[8,128]{1,0:T(8,128)S(1)}, f32[8,128]{1,0:T(8,128)S(1)}, u32[]{:S(2)}, u32[]{:S(2)}) collective-permute-start(f32[8,128]{1,0:T(8,128)S(1)} %get-tuple-element.21), channel_id=1, source_target_pairs={{1,0},{2,1},{3,2},{4,3},{5,4},{6,5},{7,6},{9,8},{10,9},{11,10},{12... | collective-permute-start | bytes 12296 | tf_op jit(solution)/shard_map/ppermute | solution.py:620
  61.4 10.5 %all-to-all-start.2 = ((f32[32,4,128]{2,1,0:T(4,128)}), f32[32,4,128]{2,1,0:T(4,128)S(1)}, u32[]{:S(2)}, u32[]{:S(2)}) async-start(f32[32,4,128]{2,1,0:T(4,128)} %bitcast.7), calls=%async_computation.2 | async-start | bytes 131072 | tf_op jit(solution)/shard_map/all_to_all | solution.py:576
